TPU v7x, 512 devices: a whole 4x4x16 slice. The times are simulated.
512 devices in a mesh: expert: 64 (over x, z), tensor: 8 (over y, core).
Axes of the slice: x: 4, y: 4, z: 16, core: 2. Of those that a mesh axis runs over, the one named last changes fastest.
Arguments:
- first_half: bfloat16 [8192, 2048], P('expert', 'tensor'), may hold values from -6 to 6
- second_half: bfloat16 [8192, 2048], P('expert', 'tensor'), may hold values from -1.5 to 1.5
- first_grad: bfloat16 [8192, 2048], P('expert', 'tensor'), may hold values from -1.5 to 1.5
- second_grad: bfloat16 [8192, 2048], P('expert', 'tensor'), may hold values from -6 to 6
- expert_ids: int32 [8192, 6], P('expert'), may hold values from 0 to 63, as said below
- gate_weights: bfloat16 [8192, 6], P('expert'), may hold values from 0.049804688 to 0.5
- expert_in: bfloat16 [64, 2, 1408, 2048], P('expert', None, 'tensor'), may hold values from -0.125 to 0.125
- expert_out: bfloat16 [64, 1408, 2048], P('expert', 'tensor'), may hold values from -0.15625 to 0.15625
Outputs:
- restored: bfloat16 [8192, 2048], P('expert', 'tensor')
- carried_grad: bfloat16 [8192, 2048], P('expert', 'tensor')
- gate_grad: float32 [8192, 6], P('expert')
- grad_in: bfloat16 [64, 2, 1408, 2048], P('expert', None, 'tensor')
- grad_out: bfloat16 [64, 1408, 2048], P('expert', 'tensor')
Inputs may be any that keep to these rules, and one draw needn't show every extreme that they name: `expert_ids`: each token names 6 different experts. In the rows of one index of expert (128 tokens) each expert is named by at least 10 and at most 14 tokens, and one expert is named by exactly 14 tokens of every index of expert.
All inputs are finite; a program needn't handle non-finite values.
Results may differ from a plain program's by a relative error of at most 0.02.
Values may be sent and summed in bfloat16 or wider, within the bound.
A program may use at most 128 MiB of HBM per device.

v0:
```python
import jax
import jax.numpy as jnp
from jax import lax
from jax.sharding import PartitionSpec as P


def expert_work(slot_rows, slot_cots, slot_gates, weights_in, weights_out):
    pre = jnp.einsum("erd,ekhd->ekrh", slot_rows, weights_in, preferred_element_type=jnp.float32)
    gate_pre = pre[:, 0]
    up_pre = pre[:, 1]
    sigma = jax.nn.sigmoid(gate_pre)
    active = gate_pre * sigma
    hidden = (active * up_pre).astype(jnp.bfloat16)
    part_out = jnp.einsum("erh,ehd->erd", hidden, weights_out, preferred_element_type=jnp.float32)
    gate_piece = jnp.sum(slot_cots.astype(jnp.float32) * part_out, axis=2)
    scaled = (slot_gates[:, :, None].astype(jnp.float32) * slot_cots.astype(jnp.float32)).astype(
        jnp.bfloat16
    )
    hidden_grad = jnp.einsum(
        "erd,ehd->erh", scaled, weights_out, preferred_element_type=jnp.float32
    )
    gate_pre_grad = (hidden_grad * up_pre * sigma * (1.0 + gate_pre * (1.0 - sigma))).astype(
        jnp.bfloat16
    )
    up_grad = (hidden_grad * active).astype(jnp.bfloat16)
    input_piece = jnp.einsum(
        "erh,ehd->erd", gate_pre_grad, weights_in[:, 0], preferred_element_type=jnp.float32
    ) + jnp.einsum("erh,ehd->erd", up_grad, weights_in[:, 1], preferred_element_type=jnp.float32)
    grad_gate = jnp.einsum(
        "erh,erd->ehd", gate_pre_grad, slot_rows, preferred_element_type=jnp.float32
    ).astype(jnp.bfloat16)
    grad_up = jnp.einsum(
        "erh,erd->ehd", up_grad, slot_rows, preferred_element_type=jnp.float32
    ).astype(jnp.bfloat16)
    grad_in = jnp.stack([grad_gate, grad_up], axis=1)
    grad_out = jnp.einsum(
        "erh,erd->ehd", hidden, scaled, preferred_element_type=jnp.float32
    ).astype(jnp.bfloat16)
    return (part_out, input_piece, gate_piece, grad_in, grad_out)


def body(
    first_half,
    second_half,
    first_grad,
    second_grad,
    expert_ids,
    gate_weights,
    expert_in,
    expert_out,
):
    tokens_here = expert_ids.shape[0]
    picks = expert_ids.shape[1]
    groups = lax.axis_size("expert")
    local_count = expert_in.shape[0]
    experts_all = groups * local_count
    capacity = tokens_here * picks * 7 // (6 * experts_all)
    routes = expert_ids.reshape(-1)
    onehot = (routes[:, None] == jnp.arange(experts_all, dtype=jnp.int32)[None, :]).astype(
        jnp.int32
    )
    before = jnp.cumsum(onehot, axis=0) - onehot
    slot_index = jnp.sum(before * onehot, axis=1)
    destination = routes * capacity + slot_index
    route_token = jnp.arange(tokens_here * picks, dtype=jnp.int32) // picks
    slot_token = (
        jnp.full((experts_all * capacity,), tokens_here, jnp.int32).at[destination].set(route_token)
    )
    slot_gate = (
        jnp.zeros((experts_all * capacity,), jnp.bfloat16)
        .at[destination]
        .set(gate_weights.reshape(-1))
    )
    slot_gate = slot_gate.reshape(experts_all, capacity)

    def to_slots(values):
        padded = jnp.concatenate([values, jnp.zeros((1, values.shape[1]), values.dtype)], axis=0)
        return padded[slot_token].reshape(experts_all, capacity, values.shape[1])

    def to_local(values):
        shaped = values.reshape((groups, local_count) + values.shape[1:])
        shaped = jnp.moveaxis(shaped, 1, 0)
        return shaped.reshape((local_count, groups * capacity) + values.shape[2:])

    def to_sources(values):
        shaped = values.reshape((local_count, groups, capacity) + values.shape[2:])
        shaped = jnp.moveaxis(shaped, 0, 1)
        return shaped.reshape((experts_all, capacity) + values.shape[2:])

    whole_first, whole_cots = (
        lax.all_gather(first_half, "tensor", axis=1, tiled=True),
        lax.all_gather(second_grad, "tensor", axis=1, tiled=True),
    )
    recv_rows, recv_cots, recv_gates = (
        lax.all_to_all(to_slots(whole_first), "expert", split_axis=0, concat_axis=0, tiled=True),
        lax.all_to_all(to_slots(whole_cots), "expert", split_axis=0, concat_axis=0, tiled=True),
        lax.all_to_all(slot_gate, "expert", split_axis=0, concat_axis=0, tiled=True),
    )
    results = expert_work(
        to_local(recv_rows), to_local(recv_cots), to_local(recv_gates), expert_in, expert_out
    )
    grad_in = results[3]
    grad_out = results[4]
    gate_all = to_sources(results[2]).astype(jnp.bfloat16)
    weights_f = gate_weights.astype(jnp.float32)
    out_all = to_sources(results[0].astype(jnp.bfloat16))
    input_all = to_sources(results[1].astype(jnp.bfloat16))
    back_out, back_input, back_gate = (
        lax.all_to_all(out_all, "expert", split_axis=0, concat_axis=0, tiled=True),
        lax.all_to_all(input_all, "expert", split_axis=0, concat_axis=0, tiled=True),
        lax.all_to_all(gate_all, "expert", split_axis=0, concat_axis=0, tiled=True),
    )
    width = back_out.shape[2]
    picked_out = back_out.reshape(-1, width)[destination].reshape(tokens_here, picks, width)
    picked_input = back_input.reshape(-1, width)[destination].reshape(tokens_here, picks, width)
    mixed = jnp.sum(weights_f[:, :, None] * picked_out.astype(jnp.float32), axis=1)
    summed_input = jnp.sum(picked_input.astype(jnp.float32), axis=1)
    branch_cols, input_cols = (
        lax.psum_scatter(
            mixed.astype(jnp.bfloat16), "tensor", scatter_dimension=1, tiled=True
        ).astype(jnp.float32),
        lax.psum_scatter(
            summed_input.astype(jnp.bfloat16), "tensor", scatter_dimension=1, tiled=True
        ).astype(jnp.float32),
    )
    gate_back = back_gate.astype(jnp.float32)
    gate_parts = gate_back.reshape(-1)[destination].reshape(tokens_here, picks)
    gate_grad = lax.psum(gate_parts, "tensor")
    restored = (second_half.astype(jnp.float32) - branch_cols).astype(jnp.bfloat16)
    carried_grad = (first_grad.astype(jnp.float32) + input_cols).astype(jnp.bfloat16)
    return (restored, carried_grad, gate_grad, grad_in, grad_out)


def solution(mesh):
    in_specs = (
        P("expert", "tensor"),
        P("expert", "tensor"),
        P("expert", "tensor"),
        P("expert", "tensor"),
        P("expert", None),
        P("expert", None),
        P("expert", None, "tensor", None),
        P("expert", "tensor", None),
    )
    out_specs = (
        P("expert", "tensor"),
        P("expert", "tensor"),
        P("expert", None),
        P("expert", None, "tensor", None),
        P("expert", "tensor", None),
    )
    return jax.shard_map(body, mesh=mesh, in_specs=in_specs, out_specs=out_specs, check_vma=False)
```

profile of v0, /device:TPU:2, one launch (start us, length us, event | category | flops | bytes accessed | tf_op | source)
XLA Modules:
  0.0 958.2 jit_solution(17557005658640460501)
XLA Ops:
  9.3 1.8 reduce-window.6
  11.6 3.4 scatter_custom_fusion
  15.0 13.8 %all_gather.6 = bf16[128,2048]{1,0:T(8,128)(2,1)S(1)} all-gather(bf16[128,256]{1,0:T(8,128)(2,1)} %param.8), channel_id=1, replica_groups=mesh['expert'=64,'tensor'=8] {'tensor'}, dimensions={1}, use_global_device_ids=true | all-gather | bytes 589824 | tf_op jit(solution)/shard_map/all_gather | solution.py:91
  28.9 5.0 gather_fusion
  33.9 6.0 reshape.268
  39.9 19.0 %all-to-all-start = ((bf16[64,14,2048]{2,1,0:T(8,128)(2,1)}), bf16[64,14,2048]{2,1,0:T(8,128)(2,1)}, u32[]{:S(2)}, u32[]{:S(2)}) async-start(bf16[64,14,2048]{2,1,0:T(8,128)(2,1)} %reshape.268), calls=%async_computation | async-start | bytes 8388608 | tf_op jit(solution)/shard_map/all_to_all | solution.py:95
  58.9 13.1 %all_gather.7 = bf16[128,2048]{1,0:T(8,128)(2,1)S(1)} all-gather(bf16[128,256]{1,0:T(8,128)(2,1)S(1)} %copy-done.4), channel_id=1, replica_groups=mesh['expert'=64,'tensor'=8] {'tensor'}, dimensions={1}, use_global_device_ids=true | all-gather | bytes 589824 | tf_op jit(solution)/shard_map/all_gather | solution.py:92
  72.0 5.1 gather_fusion.2
  77.1 6.0 reshape.274
  83.1 162.1 %all-to-all-done = bf16[64,14,2048]{2,1,0:T(8,128)(2,1)} async-done(((bf16[64,14,2048]{2,1,0:T(8,128)(2,1)}), bf16[64,14,2048]{2,1,0:T(8,128)(2,1)}, u32[]{:S(2)}, u32[]{:S(2)}) %all-to-all-start) | async-done | bytes 3670048 | tf_op jit(solution)/shard_map/all_to_all | solution.py:95
  245.2 10.5 %all-to-all-start.3 = ((bf16[64,14,2048]{2,1,0:T(8,128)(2,1)}), bf16[64,14,2048]{2,1,0:T(8,128)(2,1)}, u32[]{:S(2)}, u32[]{:S(2)}) async-start(bf16[64,14,2048]{2,1,0:T(8,128)(2,1)} %reshape.274), calls=%async_computation.4 | async-start | bytes 8388608 | tf_op jit(solution)/shard_map/all_to_all | solution.py:96
  256.0 8.6 scatter_custom_fusion.1
  265.4 6.1 reshape.343
  271.5 3.7 fusion.6
  275.2 1.0 copy-done.3
  276.4 164.4 %all-to-all-done.3 = bf16[64,14,2048]{2,1,0:T(8,128)(2,1)} async-done(((bf16[64,14,2048]{2,1,0:T(8,128)(2,1)}), bf16[64,14,2048]{2,1,0:T(8,128)(2,1)}, u32[]{:S(2)}, u32[]{:S(2)}) %all-to-all-start.3) | async-done | bytes 3670048 | tf_op jit(solution)/shard_map/all_to_all | solution.py:96
  440.8 9.9 %all-to-all-start.2 = ((bf16[64,1,14]{2,1,0:T(2,128)(2,1)}), bf16[64,1,14]{2,1,0:T(2,128)(2,1)S(1)}, u32[]{:S(2)}, u32[]{:S(2)}) async-start(bf16[64,1,14]{2,1,0:T(2,128)(2,1)} %all_to_all.29), calls=%async_computation.3 | async-start | bytes 65536 | tf_op jit(solution)/shard_map/all_to_all | solution.py:97
  450.7 6.5 reshape.283
  457.1 6.1 multiply_reduce_fusion.1
  463.3 6.0 reshape_transpose_reshape.4
  469.3 15.7 %all-to-all-start.1 = ((bf16[64,14,2048]{2,1,0:T(8,128)(2,1)}), bf16[64,14,2048]{2,1,0:T(8,128)(2,1)}, u32[]{:S(2)}, u32[]{:S(2)}) async-start(bf16[64,14,2048]{2,1,0:T(8,128)(2,1)} %reshape_transpose_reshape.4), calls=%async_computation.1 | async-start | bytes 8388608 | tf_op jit(solution)/shard_map/all_to_all | solution.py:109
  485.2 6.4 reshape.282
  491.6 4.9 fusion.25
  496.5 1.2 fusion.10
  497.6 3.1 add_convert_fusion
  500.7 6.0 reshape_transpose_reshape.10
  506.8 162.8 %all-to-all-done.1 = bf16[64,14,2048]{2,1,0:T(8,128)(2,1)} async-done(((bf16[64,14,2048]{2,1,0:T(8,128)(2,1)}), bf16[64,14,2048]{2,1,0:T(8,128)(2,1)}, u32[]{:S(2)}, u32[]{:S(2)}) %all-to-all-start.1) | async-done | bytes 3670048 | tf_op jit(solution)/shard_map/all_to_all | solution.py:109
  669.5 10.1 %all-to-all-start.4 = ((bf16[64,14,2048]{2,1,0:T(8,128)(2,1)}), bf16[64,14,2048]{2,1,0:T(8,128)(2,1)}, u32[]{:S(2)}, u32[]{:S(2)}) async-start(bf16[64,14,2048]{2,1,0:T(8,128)(2,1)} %reshape_transpose_reshape.10), calls=%async_computation.5 | async-start | bytes 8388608 | tf_op jit(solution)/shard_map/all_to_all | solution.py:110
  679.8 6.0 reshape.272
  685.8 9.6 %gather_fusion.1 = bf16[768,2048]{1,0:T(8,128)(2,1)} fusion(bf16[896,2048]{1,0:T(8,128)(2,1)} %reshape.272, s32[1024]{0:T(1024)S(1)} %pad_clamp_fusion), kind=kCustom, calls=%fused_computation.1 | custom fusion | bytes 6294528 | tf_op jit(solution)/shard_map/gather | solution.py:114
  695.4 6.6 reshape.280
  702.0 7.4 multiply_reduce_fusion
  709.6 6.0 reshape.269
  715.6 3.0 fusion.2
  718.6 146.4 %all-to-all-done.4 = bf16[64,14,2048]{2,1,0:T(8,128)(2,1)} async-done(((bf16[64,14,2048]{2,1,0:T(8,128)(2,1)}), bf16[64,14,2048]{2,1,0:T(8,128)(2,1)}, u32[]{:S(2)}, u32[]{:S(2)}) %all-to-all-start.4) | async-done | bytes 3670048 | tf_op jit(solution)/shard_map/all_to_all | solution.py:110
  865.1 6.0 reshape.277
  871.1 9.7 %gather_fusion.3 = bf16[768,2048]{1,0:T(8,128)(2,1)} fusion(bf16[896,2048]{1,0:T(8,128)(2,1)} %reshape.277, s32[1024]{0:T(1024)S(1)} %pad_clamp_fusion), kind=kCustom, calls=%fused_computation.3 | custom fusion | bytes 6294528 | tf_op jit(solution)/shard_map/gather | solution.py:115
  880.7 6.3 reshape.278
  887.0 5.7 reduce_sum.44
  892.7 3.0 fusion.1
  896.5 10.0 %all-to-all-start.5 = ((bf16[64,1,14]{2,1,0:T(2,128)(2,1)}), bf16[64,1,14]{2,1,0:T(2,128)(2,1)S(1)}, u32[]{:S(2)}, u32[]{:S(2)}) async-start(bf16[64,1,14]{2,1,0:T(2,128)(2,1)} %convert_element_type.209), calls=%async_computation.7 | async-start | bytes 65536 | tf_op jit(solution)/shard_map/all_to_all | solution.py:111
  906.5 5.0 fusion.3
  911.5 1.2 pad_maximum_fusion
  912.7 7.2 all-to-all-done.5
  920.1 3.2 gather_fusion.4
  923.5 24.0 %psum.7 = f32[128,6]{1,0:T(8,128)S(1)} all-reduce(f32[128,6]{1,0:T(8,128)S(1)} %reshape.279), channel_id=1, replica_groups=mesh['expert'=64,'tensor'=8] {'tensor'}, use_global_device_ids=true, to_apply=%region_10.11 | all-reduce | flops 768 | bytes 6144 | tf_op jit(solution)/shard_map/psum | solution.py:128
  948.1 1.5 subtract_convert_fusion
  949.6 1.5 add_convert_fusion.1
  (51 shorter events, 6.4 us)
Async XLA Ops:
  7.2 450.0 %copy-start = (bf16[1,176,2048]{2,1,0:T(8,128)(2,1)S(1)}, bf16[1,176,2048]{2,1,0:T(8,128)(2,1)}, u32[]{:S(2)}) copy-start(bf16[1,176,2048]{2,1,0:T(8,128)(2,1)} %param.15) | copy-start | bytes 2162692
  39.9 19.0 %copy-start.4 = (bf16[128,256]{1,0:T(8,128)(2,1)S(1)}, bf16[128,256]{1,0:T(8,128)(2,1)}, u32[]{:S(2)}) copy-start(bf16[128,256]{1,0:T(8,128)(2,1)} %param.11) | copy-start | bytes 196612
  39.9 205.3 %all-to-all-start = ((bf16[64,14,2048]{2,1,0:T(8,128)(2,1)}), bf16[64,14,2048]{2,1,0:T(8,128)(2,1)}, u32[]{:S(2)}, u32[]{:S(2)}) async-start(bf16[64,14,2048]{2,1,0:T(8,128)(2,1)} %reshape.268), calls=%async_computation | async-start | bytes 8388608 | tf_op jit(solution)/shard_map/all_to_all | solution.py:95
  83.1 172.6 %copy-start.7 = (bf16[128,6]{0,1:T(8,128)(2,1)S(1)}, bf16[128,6]{0,1:T(8,128)(2,1)}, u32[]{:S(2)}) copy-start(bf16[128,6]{0,1:T(8,128)(2,1)} %param.13) | copy-start | bytes 4612
  245.2 195.6 %all-to-all-start.3 = ((bf16[64,14,2048]{2,1,0:T(8,128)(2,1)}), bf16[64,14,2048]{2,1,0:T(8,128)(2,1)}, u32[]{:S(2)}, u32[]{:S(2)}) async-start(bf16[64,14,2048]{2,1,0:T(8,128)(2,1)} %reshape.274), calls=%async_computation.4 | async-start | bytes 8388608 | tf_op jit(solution)/shard_map/all_to_all | solution.py:96
  265.4 6.1 copy-start.2
  275.2 1.0 copy-start.3
  440.8 28.5 %all-to-all-start.2 = ((bf16[64,1,14]{2,1,0:T(2,128)(2,1)}), bf16[64,1,14]{2,1,0:T(2,128)(2,1)S(1)}, u32[]{:S(2)}, u32[]{:S(2)}) async-start(bf16[64,1,14]{2,1,0:T(2,128)(2,1)} %all_to_all.29), calls=%async_computation.3 | async-start | bytes 65536 | tf_op jit(solution)/shard_map/all_to_all | solution.py:97
  469.3 200.3 %all-to-all-start.1 = ((bf16[64,14,2048]{2,1,0:T(8,128)(2,1)}), bf16[64,14,2048]{2,1,0:T(8,128)(2,1)}, u32[]{:S(2)}, u32[]{:S(2)}) async-start(bf16[64,14,2048]{2,1,0:T(8,128)(2,1)} %reshape_transpose_reshape.4), calls=%async_computation.1 | async-start | bytes 8388608 | tf_op jit(solution)/shard_map/all_to_all | solution.py:109
  669.5 195.5 %all-to-all-start.4 = ((bf16[64,14,2048]{2,1,0:T(8,128)(2,1)}), bf16[64,14,2048]{2,1,0:T(8,128)(2,1)}, u32[]{:S(2)}, u32[]{:S(2)}) async-start(bf16[64,14,2048]{2,1,0:T(8,128)(2,1)} %reshape_transpose_reshape.10), calls=%async_computation.5 | async-start | bytes 8388608 | tf_op jit(solution)/shard_map/all_to_all | solution.py:110
  679.6 268.5 %reduce-scatter.3.cloned.1.call-start = ((), (), s32[]{:S(2)}) async-start(), calls=%async_computation.8 | async-start | bytes 589824 | tf_op jit(solution)/shard_map/reduce_scatter | solution.py:119
  709.4 240.3 %reduce-scatter.5.cloned.1.call-start = ((), (), s32[]{:S(2)}) async-start(), calls=%async_computation.9 | async-start | bytes 589824 | tf_op jit(solution)/shard_map/reduce_scatter | solution.py:122
  896.5 23.4 %all-to-all-start.5 = ((bf16[64,1,14]{2,1,0:T(2,128)(2,1)}), bf16[64,1,14]{2,1,0:T(2,128)(2,1)S(1)}, u32[]{:S(2)}, u32[]{:S(2)}) async-start(bf16[64,1,14]{2,1,0:T(2,128)(2,1)} %convert_element_type.209), calls=%async_computation.7 | async-start | bytes 65536 | tf_op jit(solution)/shard_map/all_to_all | solution.py:111
  906.4 44.7 %copy-start.1 = (bf16[1,176,2048]{2,1,0:T(8,128)(2,1)S(1)}, bf16[1,176,2048]{2,1,0:T(8,128)(2,1)}, u32[]{:S(2)}) copy-start(bf16[1,176,2048]{2,1,0:T(8,128)(2,1)} %param.15) | copy-start | bytes 2162692
  911.5 36.7 %copy-start.5 = (bf16[128,256]{1,0:T(8,128)(2,1)S(1)}, bf16[128,256]{1,0:T(8,128)(2,1)}, u32[]{:S(2)}) copy-start(bf16[128,256]{1,0:T(8,128)(2,1)} %param.9) | copy-start | bytes 196612
  911.5 38.1 %copy-start.6 = (bf16[128,256]{1,0:T(8,128)(2,1)S(1)}, bf16[128,256]{1,0:T(8,128)(2,1)}, u32[]{:S(2)}) copy-start(bf16[128,256]{1,0:T(8,128)(2,1)} %param.10) | copy-start | bytes 196612
Sparse Core Ops, SparseCore 0:
  709.5 39.6 reduce-scatter.2
  892.8 34.0 reduce-scatter.4
where the time goes:
time: 967 us; the launch traced here: 958 us
  waiting for transfers between devices  643 us (66%)
  local copies, waits for them, and re-layouts  124 us (13%)
  starting transfers between devices  75.4 us (8%)
  blocking collectives  50.9 us (5%)
  matrix products  30 us (3%)
  other arithmetic  20.4 us (2%)
  between operations  14.6 us (2%)
    all_to_all x1, waiting for transfers between devices, body(): lax.all_to_all(to_slots(whole_cots), 'expert', split_axis=0, concat_axis=...  164 us
    all_to_all x1, waiting for transfers between devices, body(): lax.all_to_all(out_all, 'expert', split_axis=0, concat_axis=0, tiled=True)  163 us
    all_to_all x1, waiting for transfers between devices, body(): lax.all_to_all(to_slots(whole_first), 'expert', split_axis=0, concat_axis...  162 us
    all_to_all x1, waiting for transfers between devices, body(): lax.all_to_all(input_all, 'expert', split_axis=0, concat_axis=0, tiled=True)  146 us
    psum x1, blocking collectives, body(): gate_grad = lax.psum(gate_parts, 'tensor')  24 us
  transfers between devices with their start and end apart: 8, of which 5 were waited for; matrix products, arithmetic and copies ran while one was open for 16% of the time, Pallas kernels for 0%

commit v1 on v0

--- a/solution.py
+++ b/solution.py
@@ -2,6 +2,15 @@
 import jax.numpy as jnp
 from jax import lax
 from jax.sharding import PartitionSpec as P
+
+
+def doubling_sum(x, mesh_axis):
+    n_dev = lax.axis_size(mesh_axis)
+    acc, far = (x, 1)
+    while far < n_dev:
+        acc = acc + lax.ppermute(acc, mesh_axis, [(i, i ^ far) for i in range(n_dev)])
+        far = 2 * far
+    return acc
 
 
 def expert_work(slot_rows, slot_cots, slot_gates, weights_in, weights_out):
@@ -125,7 +134,7 @@
     )
     gate_back = back_gate.astype(jnp.float32)
     gate_parts = gate_back.reshape(-1)[destination].reshape(tokens_here, picks)
-    gate_grad = lax.psum(gate_parts, "tensor")
+    gate_grad = doubling_sum(gate_parts, "tensor")
     restored = (second_half.astype(jnp.float32) - branch_cols).astype(jnp.bfloat16)
     carried_grad = (first_grad.astype(jnp.float32) + input_cols).astype(jnp.bfloat16)
     return (restored, carried_grad, gate_grad, grad_in, grad_out)

time: 967 us -> 959 us (level)
  the two profiles are of different devices: /device:TPU:2 before, /device:TPU:6 now
where the time goes in v1:
time: 959 us; the launch traced here: 951 us
  waiting for transfers between devices  654 us (68%)
  local copies, waits for them, and re-layouts  124 us (13%)
  starting transfers between devices  83.1 us (9%)
  matrix products  28 us (3%)
  blocking collectives  27 us (3%)
  other arithmetic  20.5 us (2%)
  between operations  14.6 us (2%)
    all_to_all x1, waiting for transfers between devices, body(): lax.all_to_all(to_slots(whole_cots), 'expert', split_axis=0, concat_axis=...  165 us
    all_to_all x1, waiting for transfers between devices, body(): lax.all_to_all(out_all, 'expert', split_axis=0, concat_axis=0, tiled=True)  162 us
    all_to_all x1, waiting for transfers between devices, body(): lax.all_to_all(to_slots(whole_first), 'expert', split_axis=0, concat_axis...  162 us
    all_to_all x1, waiting for transfers between devices, body(): lax.all_to_all(input_all, 'expert', split_axis=0, concat_axis=0, tiled=True)  139 us
  transfers between devices with their start and end apart: 11, of which 8 were waited for; matrix products, arithmetic and copies ran while one was open for 16% of the time, Pallas kernels for 0%

profile of v1, /device:TPU:6, one launch (start us, length us, event | category | flops | bytes accessed | tf_op | source)
XLA Modules:
  0.0 951.1 jit_solution(7592759160706919970)
XLA Ops:
  9.3 1.8 reduce-window.6
  11.6 3.4 scatter_custom_fusion
  15.0 13.8 %all_gather.6 = bf16[128,2048]{1,0:T(8,128)(2,1)S(1)} all-gather(bf16[128,256]{1,0:T(8,128)(2,1)} %param.8), channel_id=1, replica_groups=mesh['expert'=64,'tensor'=8] {'tensor'}, dimensions={1}, use_global_device_ids=true | all-gather | bytes 589824 | tf_op jit(solution)/shard_map/all_gather | solution.py:100
  28.9 5.0 gather_fusion
  33.9 6.0 reshape.268
  39.9 19.1 %all-to-all-start = ((bf16[64,14,2048]{2,1,0:T(8,128)(2,1)}), bf16[64,14,2048]{2,1,0:T(8,128)(2,1)}, u32[]{:S(2)}, u32[]{:S(2)}) async-start(bf16[64,14,2048]{2,1,0:T(8,128)(2,1)} %reshape.268), calls=%async_computation | async-start | bytes 8388608 | tf_op jit(solution)/shard_map/all_to_all | solution.py:104
  59.0 13.1 %all_gather.7 = bf16[128,2048]{1,0:T(8,128)(2,1)S(1)} all-gather(bf16[128,256]{1,0:T(8,128)(2,1)S(1)} %copy-done.5), channel_id=1, replica_groups=mesh['expert'=64,'tensor'=8] {'tensor'}, dimensions={1}, use_global_device_ids=true | all-gather | bytes 589824 | tf_op jit(solution)/shard_map/all_gather | solution.py:101
  72.2 5.1 gather_fusion.2
  77.2 6.0 reshape.274
  83.3 162.1 %all-to-all-done = bf16[64,14,2048]{2,1,0:T(8,128)(2,1)} async-done(((bf16[64,14,2048]{2,1,0:T(8,128)(2,1)}), bf16[64,14,2048]{2,1,0:T(8,128)(2,1)}, u32[]{:S(2)}, u32[]{:S(2)}) %all-to-all-start) | async-done | bytes 3670048 | tf_op jit(solution)/shard_map/all_to_all | solution.py:104
  245.4 10.5 %all-to-all-start.3 = ((bf16[64,14,2048]{2,1,0:T(8,128)(2,1)}), bf16[64,14,2048]{2,1,0:T(8,128)(2,1)}, u32[]{:S(2)}, u32[]{:S(2)}) async-start(bf16[64,14,2048]{2,1,0:T(8,128)(2,1)} %reshape.274), calls=%async_computation.4 | async-start | bytes 8388608 | tf_op jit(solution)/shard_map/all_to_all | solution.py:105
  256.1 8.6 scatter_custom_fusion.1
  265.5 6.1 reshape.343
  271.6 3.7 fusion.6
  276.6 164.6 %all-to-all-done.3 = bf16[64,14,2048]{2,1,0:T(8,128)(2,1)} async-done(((bf16[64,14,2048]{2,1,0:T(8,128)(2,1)}), bf16[64,14,2048]{2,1,0:T(8,128)(2,1)}, u32[]{:S(2)}, u32[]{:S(2)}) %all-to-all-start.3) | async-done | bytes 3670048 | tf_op jit(solution)/shard_map/all_to_all | solution.py:105
  441.1 9.6 %all-to-all-start.2 = ((bf16[64,1,14]{2,1,0:T(2,128)(2,1)}), bf16[64,1,14]{2,1,0:T(2,128)(2,1)S(1)}, u32[]{:S(2)}, u32[]{:S(2)}) async-start(bf16[64,1,14]{2,1,0:T(2,128)(2,1)} %all_to_all.29), calls=%async_computation.3 | async-start | bytes 65536 | tf_op jit(solution)/shard_map/all_to_all | solution.py:106
  450.8 6.5 reshape.283
  457.3 6.1 multiply_reduce_fusion.1
  464.2 15.1 %all-to-all-start.5 = ((bf16[64,1,14]{2,1,0:T(2,128)(2,1)}), bf16[64,1,14]{2,1,0:T(2,128)(2,1)S(1)}, u32[]{:S(2)}, u32[]{:S(2)}) async-start(bf16[64,1,14]{2,1,0:T(2,128)(2,1)} %convert_element_type.209), calls=%async_computation.7 | async-start | bytes 65536 | tf_op jit(solution)/shard_map/all_to_all | solution.py:120
  479.3 6.0 reshape_transpose_reshape.4
  485.3 6.5 all-to-all-done.5
  491.8 9.2 all-to-all-start.1
  501.3 6.4 reshape.282
  507.7 4.8 fusion.25
  513.7 3.1 add_convert_fusion
  516.8 6.0 reshape_transpose_reshape.10
  522.8 162.3 %all-to-all-done.1 = bf16[64,14,2048]{2,1,0:T(8,128)(2,1)} async-done(((bf16[64,14,2048]{2,1,0:T(8,128)(2,1)}), bf16[64,14,2048]{2,1,0:T(8,128)(2,1)}, u32[]{:S(2)}, u32[]{:S(2)}) %all-to-all-start.1) | async-done | bytes 3670048 | tf_op jit(solution)/shard_map/all_to_all | solution.py:118
  685.1 10.0 %all-to-all-start.4 = ((bf16[64,14,2048]{2,1,0:T(8,128)(2,1)}), bf16[64,14,2048]{2,1,0:T(8,128)(2,1)}, u32[]{:S(2)}, u32[]{:S(2)}) async-start(bf16[64,14,2048]{2,1,0:T(8,128)(2,1)} %reshape_transpose_reshape.10), calls=%async_computation.5 | async-start | bytes 8388608 | tf_op jit(solution)/shard_map/all_to_all | solution.py:119
  695.3 6.0 reshape.272
  701.3 9.6 %gather_fusion.1 = bf16[768,2048]{1,0:T(8,128)(2,1)} fusion(bf16[896,2048]{1,0:T(8,128)(2,1)} %reshape.272, s32[1024]{0:T(1024)S(1)} %pad_clamp_fusion), kind=kCustom, calls=%fused_computation.1 | custom fusion | bytes 6294528 | tf_op jit(solution)/shard_map/gather | solution.py:123
  710.9 6.6 reshape.280
  717.5 7.4 multiply_reduce_fusion
  725.1 6.0 reshape.269
  731.1 4.9 fusion.3
  736.3 3.2 gather_fusion.4
  739.6 1.9 collective-permute-start
  741.6 139.3 %all-to-all-done.4 = bf16[64,14,2048]{2,1,0:T(8,128)(2,1)} async-done(((bf16[64,14,2048]{2,1,0:T(8,128)(2,1)}), bf16[64,14,2048]{2,1,0:T(8,128)(2,1)}, u32[]{:S(2)}, u32[]{:S(2)}) %all-to-all-start.4) | async-done | bytes 3670048 | tf_op jit(solution)/shard_map/all_to_all | solution.py:119
  880.8 6.0 reshape.277
  886.8 9.6 %gather_fusion.3 = bf16[768,2048]{1,0:T(8,128)(2,1)} fusion(bf16[896,2048]{1,0:T(8,128)(2,1)} %reshape.277, s32[1024]{0:T(1024)S(1)} %pad_clamp_fusion), kind=kCustom, calls=%fused_computation.3 | custom fusion | bytes 6294528 | tf_op jit(solution)/shard_map/gather | solution.py:124
  896.5 6.3 reshape.278
  902.7 5.7 reduce_sum.44
  908.4 3.1 fusion.2
  911.7 3.3 collective-permute-start.1
  916.0 2.5 collective-permute-done.1
  918.4 4.0 collective-permute-start.2
  923.7 2.8 collective-permute-done.2
  927.1 1.5 subtract_convert_fusion
  928.6 13.9 %reduce-scatter.5.cloned.1.call-done = bf16[128,256]{1,0:T(8,128)(2,1)} async-done(((bf16[128,2048]{1,0:T(8,128)(2,1)}), bf16[128,256]{1,0:T(8,128)(2,1)}) %reduce-scatter.5.cloned.1.call-update) | async-done | bytes 65552 | tf_op jit(solution)/shard_map/reduce_scatter | solution.py:131
  (61 shorter events, 12.3 us)
Async XLA Ops:
  7.2 450.1 %copy-start = (bf16[1,176,2048]{2,1,0:T(8,128)(2,1)S(1)}, bf16[1,176,2048]{2,1,0:T(8,128)(2,1)}, u32[]{:S(2)}) copy-start(bf16[1,176,2048]{2,1,0:T(8,128)(2,1)} %param.15) | copy-start | bytes 2162692
  39.9 19.1 %copy-start.5 = (bf16[128,256]{1,0:T(8,128)(2,1)S(1)}, bf16[128,256]{1,0:T(8,128)(2,1)}, u32[]{:S(2)}) copy-start(bf16[128,256]{1,0:T(8,128)(2,1)} %param.11) | copy-start | bytes 196612
  39.9 205.5 %all-to-all-start = ((bf16[64,14,2048]{2,1,0:T(8,128)(2,1)}), bf16[64,14,2048]{2,1,0:T(8,128)(2,1)}, u32[]{:S(2)}, u32[]{:S(2)}) async-start(bf16[64,14,2048]{2,1,0:T(8,128)(2,1)} %reshape.268), calls=%async_computation | async-start | bytes 8388608 | tf_op jit(solution)/shard_map/all_to_all | solution.py:104
  83.2 172.6 %copy-start.8 = (bf16[128,6]{0,1:T(8,128)(2,1)S(1)}, bf16[128,6]{0,1:T(8,128)(2,1)}, u32[]{:S(2)}) copy-start(bf16[128,6]{0,1:T(8,128)(2,1)} %param.13) | copy-start | bytes 4612
  245.4 195.8 %all-to-all-start.3 = ((bf16[64,14,2048]{2,1,0:T(8,128)(2,1)}), bf16[64,14,2048]{2,1,0:T(8,128)(2,1)}, u32[]{:S(2)}, u32[]{:S(2)}) async-start(bf16[64,14,2048]{2,1,0:T(8,128)(2,1)} %reshape.274), calls=%async_computation.4 | async-start | bytes 8388608 | tf_op jit(solution)/shard_map/all_to_all | solution.py:105
  265.5 6.1 copy-start.3
  275.3 1.0 copy-start.4
  441.1 23.0 %all-to-all-start.2 = ((bf16[64,1,14]{2,1,0:T(2,128)(2,1)}), bf16[64,1,14]{2,1,0:T(2,128)(2,1)S(1)}, u32[]{:S(2)}, u32[]{:S(2)}) async-start(bf16[64,1,14]{2,1,0:T(2,128)(2,1)} %all_to_all.29), calls=%async_computation.3 | async-start | bytes 65536 | tf_op jit(solution)/shard_map/all_to_all | solution.py:106
  464.2 27.6 %all-to-all-start.5 = ((bf16[64,1,14]{2,1,0:T(2,128)(2,1)}), bf16[64,1,14]{2,1,0:T(2,128)(2,1)S(1)}, u32[]{:S(2)}, u32[]{:S(2)}) async-start(bf16[64,1,14]{2,1,0:T(2,128)(2,1)} %convert_element_type.209), calls=%async_computation.7 | async-start | bytes 65536 | tf_op jit(solution)/shard_map/all_to_all | solution.py:120
  491.8 193.3 %all-to-all-start.1 = ((bf16[64,14,2048]{2,1,0:T(8,128)(2,1)}), bf16[64,14,2048]{2,1,0:T(8,128)(2,1)}, u32[]{:S(2)}, u32[]{:S(2)}) async-start(bf16[64,14,2048]{2,1,0:T(8,128)(2,1)} %reshape_transpose_reshape.4), calls=%async_computation.1 | async-start | bytes 8388608 | tf_op jit(solution)/shard_map/all_to_all | solution.py:118
  685.1 195.7 %all-to-all-start.4 = ((bf16[64,14,2048]{2,1,0:T(8,128)(2,1)}), bf16[64,14,2048]{2,1,0:T(8,128)(2,1)}, u32[]{:S(2)}, u32[]{:S(2)}) async-start(bf16[64,14,2048]{2,1,0:T(8,128)(2,1)} %reshape_transpose_reshape.10), calls=%async_computation.5 | async-start | bytes 8388608 | tf_op jit(solution)/shard_map/all_to_all | solution.py:119
  695.1 232.0 %reduce-scatter.3.cloned.1.call-start = ((), (), s32[]{:S(2)}) async-start(), calls=%async_computation.8 | async-start | bytes 589824 | tf_op jit(solution)/shard_map/reduce_scatter | solution.py:128
  724.9 217.6 %reduce-scatter.5.cloned.1.call-start = ((), (), s32[]{:S(2)}) async-start(), calls=%async_computation.9 | async-start | bytes 589824 | tf_op jit(solution)/shard_map/reduce_scatter | solution.py:131
  739.6 172.0 %collective-permute-start = (f32[128,6]{1,0:T(8,128)S(1)}, f32[128,6]{1,0:T(8,128)S(1)}, u32[]{:S(2)}, u32[]{:S(2)}) collective-permute-start(f32[128,6]{1,0:T(8,128)S(1)} %reshape.279), channel_id=1, source_target_pairs={{0,1},{1,0},{2,3},{3,2},{4,5},{5,4},{6,7},{7,6},{8,9},{9,8},{10,11... | collective-permute-start | bytes 9224 | tf_op jit(solution)/shard_map/ppermute | solution.py:11
  908.4 6.6 copy-start.2
  911.6 32.4 %copy-start.1 = (bf16[1,176,2048]{2,1,0:T(8,128)(2,1)S(1)}, bf16[1,176,2048]{2,1,0:T(8,128)(2,1)}, u32[]{:S(2)}) copy-start(bf16[1,176,2048]{2,1,0:T(8,128)(2,1)} %param.15) | copy-start | bytes 2162692
  911.6 15.5 %copy-start.6 = (bf16[128,256]{1,0:T(8,128)(2,1)S(1)}, bf16[128,256]{1,0:T(8,128)(2,1)}, u32[]{:S(2)}) copy-start(bf16[128,256]{1,0:T(8,128)(2,1)} %param.9) | copy-start | bytes 196612
  911.6 30.9 %copy-start.7 = (bf16[128,256]{1,0:T(8,128)(2,1)S(1)}, bf16[128,256]{1,0:T(8,128)(2,1)}, u32[]{:S(2)}) copy-start(bf16[128,256]{1,0:T(8,128)(2,1)} %param.10) | copy-start | bytes 196612
  911.7 6.8 collective-permute-start.1
  918.4 8.0 collective-permute-start.2
Sparse Core Ops, SparseCore 0:
  725.0 39.5 reduce-scatter.2
  908.6 33.9 reduce-scatter.4
